TPU v7x, 32 devices: a whole 2x2x4 slice. The times are simulated.
32 devices in a mesh: section: 2 (over x), dp: 16 (over z, y, core).
Axes of the slice: x: 2, y: 2, z: 4, core: 2. Of those that a mesh axis runs over, the one named last changes fastest.
Arguments:
- patches: bfloat16 [32, 128, 768], P('dp'), may hold values from -6 to 6
- masks: int32 [32, 48, 128], P('dp'), may hold values from 0 to 1, as said below
- lead_times: int32 [32], P('dp'), may hold values from 6 to 168
- cotangent: bfloat16 [32, 128, 1024], P('dp'), may hold values from -6 to 6
- patch_weight: bfloat16 [768, 1024], replicated, may hold values from -1.5 to 1.5
- var_embed: bfloat16 [48, 1024], replicated, may hold values from -6 to 6
- attention: bfloat16 [2, 4, 1024, 1024], P('section')
- attn_vectors: bfloat16 [2, 4, 1024], P('section'), may hold values from -5 to 5
- norm_gains: bfloat16 [2, 1024], replicated, may hold values from 0.5 to 1.5
- trunk_shifts: bfloat16 [3, 1024], replicated, may hold values from -5 to 5
- mlp_in: bfloat16 [1024, 4096], replicated, may hold values from -0.1875 to 0.1875
- mlp_in_bias: bfloat16 [4096], replicated, may hold values from -3 to 3
- mlp_out: bfloat16 [4096, 1024], replicated, may hold values from -0.09375 to 0.09375
Outputs:
- activations: bfloat16 [2, 32, 128, 1024], P('section', 'dp')
- input_grad: float32 [32, 128, 768], P('dp', None, 'section')
- patch_weight_grad: float32 [768, 1024], P(('section', 'dp'))
- var_embed_grad: float32 [48, 1024], replicated
- attention_grad: float32 [2, 4096, 1024], P('section', 'dp')
- attn_vectors_grad: float32 [2, 4096], P('section', 'dp')
- norm_gains_grad: float32 [2, 1024], replicated
- trunk_shifts_grad: float32 [3, 1024], replicated
- mlp_in_grad: float32 [1024, 4096], P(None, ('section', 'dp'))
- mlp_in_bias_grad: float32 [4096], P(('section', 'dp'))
- mlp_out_grad: float32 [4096, 1024], P(('section', 'dp'))
Inputs may be any that keep to these rules, and one draw needn't show every extreme that they name: `masks`: every cell of every sample has at least one present variable; the share of present variables differs from sample to sample.
All inputs are finite; a program needn't handle non-finite values.
Results may differ from a plain program's by a relative error of at most 0.015.
Values may be sent and summed in bfloat16 or wider, within the bound.
A program may use at most 384 MiB of HBM per device.

v0:
```python
import jax
import jax.numpy as jnp
from jax import lax
from jax.sharding import PartitionSpec as P

D = 1024
HEADS = 16
HEAD = 64
FF = 4096
V = 48
PIX = 16


EPSILON = 1e-05
MASKED = -1e30
HIGHEST = lax.Precision.HIGHEST


def shortened(array):
    return jax.tree.map(lambda a: a.astype(jnp.bfloat16) if a.dtype == jnp.float32 else a, array)


def from_behind(value, axis, steps):
    count = lax.axis_size(axis)
    leading, last = (max(0, -steps), min(count, count - steps))
    return lax.ppermute(value, axis, [(source, source + steps) for source in range(leading, last)])


def layer_norm(features, gain_row, shift_row):
    row_mean = jnp.mean(features, axis=-1, keepdims=True)
    centred = features - row_mean
    spread = jnp.mean(centred * centred, axis=-1, keepdims=True)
    return centred * lax.rsqrt(spread + EPSILON) * gain_row + shift_row


def exact_gelu(inputs):
    return jax.nn.gelu(inputs, approximate=False)


def matmul(left_side, right_side):
    return jnp.dot(left_side, right_side, preferred_element_type=jnp.float32)


def matmul_tn(left_side, right_side):
    return lax.dot_general(
        left_side, right_side, (((0,), (0,)), ((), ())), preferred_element_type=jnp.float32
    )


def matmul_nt(left_side, right_side):
    return lax.dot_general(
        left_side, right_side, (((1,), (1,)), ((), ())), preferred_element_type=jnp.float32
    )


def updated(carried, changes):
    merged = dict(carried)
    merged.update(changes)
    return merged


def query_terms(layer_weights, layer_vectors):
    query_vec = matmul(layer_vectors[0][None, :], layer_weights[0])[0] + layer_vectors[1].astype(
        jnp.float32
    )
    key_wide = layer_weights[1].astype(jnp.float32).reshape(D, HEADS, HEAD)
    folded = jnp.einsum("dhk,hk->dh", key_wide, query_vec.reshape(HEADS, HEAD), precision=HIGHEST)
    return (query_vec, key_wide, folded)


def embed_block(pixel_rows, valid_cells, patch_weight, var_embed, folded_low, score_scale):
    cell_count = pixel_rows.shape[0]
    shaped = pixel_rows.reshape(cell_count, V, PIX)
    pieces = jnp.einsum(
        "tvp,vpd->tvd", shaped, patch_weight.reshape(V, PIX, D), preferred_element_type=jnp.float32
    )
    embedded = (pieces + var_embed.astype(jnp.float32)[None]).astype(jnp.bfloat16)
    scores = (
        jnp.einsum("tvd,dh->tvh", embedded, folded_low, preferred_element_type=jnp.float32)
        * score_scale
    )
    scores = jnp.where(valid_cells[:, :, None] > 0, scores, MASKED)
    weights = jax.nn.softmax(scores, axis=1)
    weights_low = weights.astype(jnp.bfloat16)
    pooled = jnp.einsum(
        "tvh,tvd->thd", weights_low, embedded, preferred_element_type=jnp.float32
    ).astype(jnp.bfloat16)
    return (shaped, embedded, weights, weights_low, pooled)


def pool_values(pooled, layer_weights, layer_vectors):
    cell_count = pooled.shape[0]
    projected = jnp.einsum(
        "thd,dhk->thk",
        pooled,
        layer_weights[2].reshape(D, HEADS, HEAD),
        preferred_element_type=jnp.float32,
    )
    return (projected.reshape(cell_count, D) + layer_vectors[2].astype(jnp.float32)).astype(
        jnp.bfloat16
    )


def front_block_back(
    pixel_rows,
    valid_cells,
    d_out,
    patch_weight,
    var_embed,
    layer_weights,
    layer_vectors,
    folded_low,
    score_scale,
):
    shaped, embedded, weights, weights_low, pooled = embed_block(
        pixel_rows, valid_cells, patch_weight, var_embed, folded_low, score_scale
    )
    values_low = pool_values(pooled, layer_weights, layer_vectors)
    cell_count = pixel_rows.shape[0]
    g_bo = jnp.sum(d_out.astype(jnp.float32), axis=0)
    g_wo = matmul_tn(values_low, d_out)
    d_values = matmul_nt(d_out, layer_weights[3])
    g_bv = jnp.sum(d_values, axis=0)
    d_values_low = d_values.astype(jnp.bfloat16).reshape(cell_count, HEADS, HEAD)
    g_wv = jnp.einsum(
        "thd,thk->dhk", pooled, d_values_low, preferred_element_type=jnp.float32
    ).reshape(D, D)
    d_pooled = jnp.einsum(
        "thk,dhk->thd",
        d_values_low,
        layer_weights[2].reshape(D, HEADS, HEAD),
        preferred_element_type=jnp.float32,
    ).astype(jnp.bfloat16)
    d_weights = jnp.einsum("thd,tvd->tvh", d_pooled, embedded, preferred_element_type=jnp.float32)
    d_embedded = jnp.einsum(
        "tvh,thd->tvd", weights_low, d_pooled, preferred_element_type=jnp.float32
    )
    d_scores = (weights * (d_weights - jnp.sum(weights * d_weights, axis=1, keepdims=True))).astype(
        jnp.bfloat16
    )
    g_folded = (
        jnp.einsum("tvd,tvh->dh", embedded, d_scores, preferred_element_type=jnp.float32)
        * score_scale
    )
    d_embedded = (
        d_embedded
        + jnp.einsum("tvh,dh->tvd", d_scores, folded_low, preferred_element_type=jnp.float32)
        * score_scale
    )
    g_var = jnp.sum(d_embedded, axis=0)
    d_embedded_low = d_embedded.astype(jnp.bfloat16)
    g_patch = jnp.einsum(
        "tvp,tvd->vpd", shaped, d_embedded_low, preferred_element_type=jnp.float32
    ).reshape(V * PIX, D)
    d_pixels = jnp.einsum(
        "tvd,vpd->tvp",
        d_embedded_low,
        patch_weight.reshape(V, PIX, D),
        preferred_element_type=jnp.float32,
    ).reshape(cell_count, V * PIX)
    return (g_wv, g_wo, g_bv, g_bo, g_folded, g_var, g_patch, d_pixels)


def layer_two(
    x_in,
    lead_hours,
    d_out,
    layer_weights,
    layer_vectors,
    norm_gains,
    trunk_shifts,
    mlp_in,
    mlp_in_bias,
    mlp_out,
):
    seq_len = x_in.shape[0]
    score_scale = HEAD ** (-0.5)
    gain_rows = norm_gains.astype(jnp.float32)
    shift_rows = trunk_shifts.astype(jnp.float32)
    vec_rows = layer_vectors.astype(jnp.float32)
    lead_scale = lead_hours.astype(jnp.float32) / 100.0
    resid_in = x_in.astype(jnp.float32) + lead_scale * shift_rows[2]
    normed, first_back = jax.vjp(layer_norm, resid_in, gain_rows[0], shift_rows[0])
    normed_low = normed.astype(jnp.bfloat16)
    queries = (
        (matmul(normed_low, layer_weights[0]) + vec_rows[0])
        .astype(jnp.bfloat16)
        .reshape(seq_len, HEADS, HEAD)
    )
    key_rows = (
        matmul(normed_low, layer_weights[1]).astype(jnp.bfloat16).reshape(seq_len, HEADS, HEAD)
    )
    value_rows = (
        (matmul(normed_low, layer_weights[2]) + vec_rows[1])
        .astype(jnp.bfloat16)
        .reshape(seq_len, HEADS, HEAD)
    )
    scores = (
        jnp.einsum("qhd,khd->hqk", queries, key_rows, preferred_element_type=jnp.float32)
        * score_scale
    )
    attn_probs = jax.nn.softmax(scores, axis=-1)
    probs_low = attn_probs.astype(jnp.bfloat16)
    mixed_heads = (
        jnp.einsum("hqk,khd->qhd", probs_low, value_rows, preferred_element_type=jnp.float32)
        .reshape(seq_len, D)
        .astype(jnp.bfloat16)
    )
    resid_mid = resid_in + matmul(mixed_heads, layer_weights[3]) + vec_rows[2]
    normed_two, second_back = jax.vjp(layer_norm, resid_mid, gain_rows[1], shift_rows[1])
    normed_two_low = normed_two.astype(jnp.bfloat16)
    hidden_pre = matmul(normed_two_low, mlp_in) + mlp_in_bias.astype(jnp.float32)
    hidden, gelu_back = jax.vjp(exact_gelu, hidden_pre)
    hidden_low = hidden.astype(jnp.bfloat16)
    produced = (resid_mid + matmul(hidden_low, mlp_out) + vec_rows[3]).astype(jnp.bfloat16)
    d_final = d_out.astype(jnp.float32)
    g_b2 = jnp.sum(d_final, axis=0)
    g_wout = matmul_tn(hidden_low, d_out)
    d_hidden = matmul_nt(d_out, mlp_out)
    d_pre = gelu_back(d_hidden)[0]
    g_bin = jnp.sum(d_pre, axis=0)
    d_pre_low = d_pre.astype(jnp.bfloat16)
    g_win = matmul_tn(normed_two_low, d_pre_low)
    d_mid_norm, g_gain_two, g_shift_two = second_back(matmul_nt(d_pre_low, mlp_in))
    d_mid = d_final + d_mid_norm
    g_bo = jnp.sum(d_mid, axis=0)
    d_mid_low = d_mid.astype(jnp.bfloat16)
    g_wo = matmul_tn(mixed_heads, d_mid_low)
    d_mixed = (
        matmul_nt(d_mid_low, layer_weights[3]).astype(jnp.bfloat16).reshape(seq_len, HEADS, HEAD)
    )
    d_probs = jnp.einsum("qhd,khd->hqk", d_mixed, value_rows, preferred_element_type=jnp.float32)
    d_values = jnp.einsum(
        "hqk,qhd->khd", probs_low, d_mixed, preferred_element_type=jnp.float32
    ).reshape(seq_len, D)
    d_scores = (
        attn_probs * (d_probs - jnp.sum(attn_probs * d_probs, axis=-1, keepdims=True))
    ).astype(jnp.bfloat16)
    d_queries = (
        jnp.einsum("hqk,khd->qhd", d_scores, key_rows, preferred_element_type=jnp.float32).reshape(
            seq_len, D
        )
        * score_scale
    )
    d_keys = (
        jnp.einsum("hqk,qhd->khd", d_scores, queries, preferred_element_type=jnp.float32).reshape(
            seq_len, D
        )
        * score_scale
    )
    g_bq = jnp.sum(d_queries, axis=0)
    g_bv = jnp.sum(d_values, axis=0)
    d_queries_low = d_queries.astype(jnp.bfloat16)
    d_keys_low = d_keys.astype(jnp.bfloat16)
    d_values_low = d_values.astype(jnp.bfloat16)
    g_wq = matmul_tn(normed_low, d_queries_low)
    g_wk = matmul_tn(normed_low, d_keys_low)
    g_wv = matmul_tn(normed_low, d_values_low)
    d_normed = (
        matmul_nt(d_queries_low, layer_weights[0])
        + matmul_nt(d_keys_low, layer_weights[1])
        + matmul_nt(d_values_low, layer_weights[2])
    )
    d_in_norm, g_gain_one, g_shift_one = first_back(d_normed)
    d_in = d_mid + d_in_norm
    g_lead = lead_scale * jnp.sum(d_in, axis=0)
    return (
        produced,
        d_in.astype(jnp.bfloat16),
        jnp.stack([g_wq, g_wk, g_wv, g_wo]),
        jnp.stack([g_bq, g_bv, g_bo, g_b2]),
        jnp.stack([g_gain_one, g_gain_two]),
        jnp.stack([g_shift_one, g_shift_two, g_lead]),
        g_win,
        g_bin,
        g_wout,
    )


def send_forward(sent_rows):
    return from_behind(shortened(sent_rows), "section", 1).astype(sent_rows.dtype)


def shards(
    patches,
    masks,
    lead_times,
    cotangent,
    patch_weight,
    var_embed,
    attention,
    attn_vectors,
    norm_gains,
    trunk_shifts,
    mlp_in,
    mlp_in_bias,
    mlp_out,
):
    micro_count, seq_len, pixel_width = patches.shape
    block_rows = min(128, seq_len)
    score_scale = HEAD ** (-0.5)
    layer_weights = attention[0]
    layer_vectors = attn_vectors[0]
    on_front = lax.axis_index("section") == 0
    empty_rows = jnp.zeros((seq_len, D), jnp.bfloat16)
    carried = {
        "attn": jnp.zeros((4, D, D), jnp.float32),
        "vec": jnp.zeros((4, D), jnp.float32),
        "u_sum": jnp.zeros((D, HEADS), jnp.float32),
        "patch": jnp.zeros((V * PIX, D), jnp.float32),
        "var": jnp.zeros((V, D), jnp.float32),
        "gains": jnp.zeros((2, D), jnp.float32),
        "shifts": jnp.zeros((3, D), jnp.float32),
        "w_in": jnp.zeros((D, FF), jnp.float32),
        "b_in": jnp.zeros((FF,), jnp.float32),
        "w_out": jnp.zeros((FF, D), jnp.float32),
        "outputs": jnp.zeros((micro_count, seq_len, D), jnp.bfloat16),
        "pixels": jnp.zeros((micro_count, seq_len, pixel_width), jnp.float32),
        "returned": jnp.zeros((micro_count, seq_len, D), jnp.bfloat16),
    }

    def front_forward(carried, mb_index):
        query_vec, key_wide, folded = query_terms(layer_weights, layer_vectors)
        folded_low = folded.astype(jnp.bfloat16)
        valid_cells = masks[mb_index, :, 0:block_rows].T
        block_parts = embed_block(
            patches[mb_index, 0:block_rows],
            valid_cells,
            patch_weight,
            var_embed,
            folded_low,
            score_scale,
        )
        values_low = pool_values(block_parts[4], layer_weights, layer_vectors)
        pieces = [
            (matmul(values_low, layer_weights[3]) + layer_vectors[3].astype(jnp.float32)).astype(
                jnp.bfloat16
            )
        ]
        produced = jnp.concatenate(pieces, axis=0)
        return (
            updated(carried, {"outputs": carried["outputs"].at[mb_index].set(produced)}),
            produced,
        )

    def front_backward(carried, mb_index, d_front):
        query_vec, key_wide, folded = query_terms(layer_weights, layer_vectors)
        folded_low = folded.astype(jnp.bfloat16)
        attn_sum = carried["attn"]
        vec_sum = carried["vec"]
        u_total = carried["u_sum"]
        var_total = carried["var"]
        patch_total = carried["patch"]
        valid_cells = masks[mb_index, :, 0:block_rows].T
        block_grads = front_block_back(
            patches[mb_index, 0:block_rows],
            valid_cells,
            d_front[0:block_rows],
            patch_weight,
            var_embed,
            layer_weights,
            layer_vectors,
            folded_low,
            score_scale,
        )
        attn_sum = attn_sum.at[2].add(block_grads[0]).at[3].add(block_grads[1])
        vec_sum = vec_sum.at[2].add(block_grads[2]).at[3].add(block_grads[3])
        u_total = u_total + block_grads[4]
        var_total = var_total + block_grads[5]
        patch_total = patch_total + block_grads[6]
        pixel_pieces = [block_grads[7]]
        pixel_grads = carried["pixels"].at[mb_index].set(jnp.concatenate(pixel_pieces, axis=0))
        return updated(
            carried,
            {
                "attn": attn_sum,
                "vec": vec_sum,
                "u_sum": u_total,
                "var": var_total,
                "patch": patch_total,
                "pixels": pixel_grads,
            },
        )

    def back_step(carried, mb_index, arriving):
        produced, d_front, attn_part, vec_part, gain_part, shift_part, g_win, g_bin, g_wout = (
            layer_two(
                arriving,
                lead_times[mb_index],
                cotangent[mb_index],
                layer_weights,
                layer_vectors,
                norm_gains,
                trunk_shifts,
                mlp_in,
                mlp_in_bias,
                mlp_out,
            )
        )
        changes = {
            "attn": carried["attn"] + attn_part,
            "vec": carried["vec"] + vec_part,
            "gains": carried["gains"] + gain_part,
            "shifts": carried["shifts"] + shift_part,
            "w_in": carried["w_in"] + g_win,
            "b_in": carried["b_in"] + g_bin,
            "w_out": carried["w_out"] + g_wout,
            "outputs": carried["outputs"].at[mb_index].set(produced),
            "returned": carried["returned"].at[mb_index].set(d_front),
        }
        return (updated(carried, changes), d_front)

    def finish_front(carried):
        query_vec, key_wide, folded = query_terms(layer_weights, layer_vectors)
        u_total = carried["u_sum"]
        d_key = (u_total[:, :, None] * query_vec.reshape(HEADS, HEAD)[None]).reshape(D, D)
        d_query_vec = jnp.einsum("dh,dhk->hk", u_total, key_wide, precision=HIGHEST).reshape(D)
        d_query_weight = layer_vectors[0].astype(jnp.float32)[:, None] * d_query_vec[None, :]
        d_query = jnp.dot(layer_weights[0].astype(jnp.float32), d_query_vec, precision=HIGHEST)
        attn_sum = carried["attn"].at[0].set(d_query_weight).at[1].set(d_key)
        vec_sum = carried["vec"].at[0].set(d_query).at[1].set(d_query_vec)
        return updated(carried, {"attn": attn_sum, "vec": vec_sum})

    arriving_act = empty_rows
    for step_number in range(micro_count + 1):

        def front_turn(inputs, step_number=step_number):
            carried, act_in = inputs
            sent_rows = empty_rows
            if step_number < micro_count:
                carried, sent_rows = front_forward(carried, step_number)
            return (carried, sent_rows)

        def back_turn(inputs, step_number=step_number):
            carried, act_in = inputs
            if step_number >= 1:
                carried, returned_rows = back_step(carried, step_number - 1, act_in)
            return (carried, empty_rows)

        carried, sent_act = lax.cond(on_front, front_turn, back_turn, (carried, arriving_act))
        if step_number < micro_count:
            arriving_act = send_forward(sent_act)
    gradients_back = from_behind(shortened(carried["returned"]), "section", -1)

    def front_all(kept_state):
        for mb_index in range(micro_count):
            kept_state = front_backward(kept_state, mb_index, gradients_back[mb_index])
        return kept_state

    carried = lax.cond(on_front, front_all, lambda kept_state: kept_state, carried)
    carried = lax.cond(on_front, finish_front, lambda kept_state: kept_state, carried)
    attn_grads, vec_grads = (
        lax.psum_scatter(
            carried["attn"].reshape(1, 4 * D, D), "dp", scatter_dimension=1, tiled=True
        ),
        lax.psum_scatter(carried["vec"].reshape(1, 4 * D), "dp", scatter_dimension=1, tiled=True),
    )
    win_grads, bin_grads, wout_grads, patch_grads = (
        lax.psum_scatter(carried["w_in"], ("section", "dp"), scatter_dimension=1, tiled=True),
        lax.psum_scatter(carried["b_in"], ("section", "dp"), scatter_dimension=0, tiled=True),
        lax.psum_scatter(carried["w_out"], ("section", "dp"), scatter_dimension=0, tiled=True),
        lax.psum_scatter(carried["patch"], ("section", "dp"), scatter_dimension=0, tiled=True),
    )
    var_grads, gain_grads, shift_grads = lax.psum(
        (carried["var"], carried["gains"], carried["shifts"]), ("section", "dp")
    )
    pixel_half = pixel_width // 2
    moved = from_behind(shortened(carried["pixels"][:, :, pixel_half:]), "section", 1)
    input_grads = jnp.where(on_front, carried["pixels"][:, :, :pixel_half], moved)
    activations = carried["outputs"][None]
    return (
        activations,
        input_grads,
        patch_grads,
        var_grads,
        attn_grads,
        vec_grads,
        gain_grads,
        shift_grads,
        win_grads,
        bin_grads,
        wout_grads,
    )


def solution(mesh):
    in_specs = (
        P("dp", None, None),
        P("dp", None, None),
        P("dp"),
        P("dp", None, None),
        P(),
        P(),
        P("section", None, None, None),
        P("section", None, None),
        P(),
        P(),
        P(),
        P(),
        P(),
    )
    out_specs = (
        P("section", "dp", None, None),
        P("dp", None, "section"),
        P(("section", "dp"), None),
        P(),
        P("section", "dp", None),
        P("section", "dp"),
        P(),
        P(),
        P(None, ("section", "dp")),
        P(("section", "dp")),
        P(("section", "dp"), None),
    )
    return jax.shard_map(shards, mesh=mesh, in_specs=in_specs, out_specs=out_specs, check_vma=False)
```

profile of v0, /device:TPU:19, one launch (start us, length us, event | category | flops | bytes accessed | tf_op | source)
XLA Modules:
  0.0 1487.7 jit_solution(12403688819763839297)
XLA Ops:
  8.1 11.5 copy.216
  19.7 8.0 conditional.5
  29.0 65.2 %collective-permute-done = bf16[128,1024]{1,0:T(8,128)(2,1)S(1)} collective-permute-done((bf16[128,1024]{1,0:T(8,128)(2,1)}, bf16[128,1024]{1,0:T(8,128)(2,1)S(1)}, u32[]{:S(2)}, u32[]{:S(2)}) %collective-permute-start) | collective-permute-done | bytes 262176 | tf_op jit(solution)/shard_map/ppermute | solution.py:26
  94.3 108.1 %conditional.6 = (f32[4,1024,1024]{2,1,0:T(8,128)}, f32[4096]{0:T(1024)S(1)}, f32[2,1024]{1,0:T(2,128)S(1)}, bf16[2,128,1024]{2,1,0:T(8,128)(2,1)}, bf16[2,128,1...) conditional(s32[]{:T(128)} %convert_element_type.423, ...), branch_computations={%region_4.26_spmd, %region_26.29_spmd} | conditional | flops 10073821184 | bytes 334224192 | solution.py:440
  94.3 11.4 copy.218
  106.1 2.1 fusion.29
  108.5 2.2 fusion.28
  110.9 2.1 fusion.27
  115.4 2.2 fusion.270
  117.9 4.9 convolution_add_fusion
  122.8 10.8 fusion.271
  133.6 3.0 multiply_reduce_fusion.2
  137.6 2.7 convolution_bitcast_fusion
  140.3 2.4 fusion.26
  149.7 8.6 pad_maximum_fusion
  162.7 6.1 fusion.31
  169.7 8.2 fusion.32
  177.9 9.9 fusion.39
  203.7 7.2 collective-permute-done.1
  210.9 117.6 %conditional.7 = (f32[4,1024,1024]{2,1,0:T(8,128)}, f32[4096]{0:T(1024)}, f32[2,1024]{1,0:T(2,128)}, bf16[2,128,1024]{2,1,0:T(8,128)(2,1)}, f32[3,1024]{1,0:T(4,...) conditional(s32[]{:T(128)} %convert_element_type.423, ...), branch_computations={%region_29.51_spmd, %region_51.0_spmd} | conditional | flops 10086679552 | bytes 384986848 | solution.py:440
  211.0 11.5 copy.220
  224.7 2.1 fusion.85
  227.0 2.2 fusion.84
  229.5 2.2 fusion.83
  234.1 2.2 fusion.277
  236.6 4.9 convolution_add_fusion.4
  241.5 10.5 fusion.278
  252.1 3.0 multiply_reduce_fusion.9
  256.1 2.6 convolution_bitcast_fusion.5
  258.7 3.1 fusion.82
  261.8 1.8 copy.178
  263.6 3.2 fusion.272
  266.8 1.9 convolution_bitcast_fusion.6
  274.7 13.3 maximum_add_fusion
  293.7 14.4 convolution_add_fusion.3
  308.1 13.7 convolution_add_fusion.2
  321.8 6.2 fusion.87
  329.9 9.6 collective-permute-done.2
  339.5 9.7 conditional.8
  339.5 2.1 broadcast_in_dim.142
  357.7 441.1 %all-reduce.3 = (f32[2,1024]{1,0:T(2,128)}, f32[3,1024]{1,0:T(4,128)}, f32[4096]{0:T(1024)S(1)}) all-reduce(f32[2,1024]{1,0:T(2,128)S(1)} %copy-done.81, f32[3,1024]{1,0:T(4,128)S(1)} %copy-done.75, f32[4096]{0:T(1024)S(1)} %copy-done.85), channel_id=1, replica_groups=mesh['section'=2,'dp'=16] {'section','dp'}, use_global_device_ids=true, to_apply=%region_72.0 | all-reduce | flops 9216 | bytes 73728 | tf_op jit(solution)/shard_map/psum | solution.py:464
  799.4 12.3 reduce-scatter.16.cloned.1.call-done
  814.0 73.4 %all-reduce.6.cloned.1.call-done = f32[48,1024]{1,0:T(8,128)} async-done(((f32[48,1024]{1,0:T(8,128)}), f32[48,1024]{1,0:T(8,128)}) %all-reduce.6.cloned.1.call-update) | async-done | bytes 196624 | tf_op jit(solution)/shard_map/psum | solution.py:464
  887.4 32.0 %reduce-scatter.8.cloned.1.call-done = f32[24,1024]{1,0:T(8,128)} async-done(((f32[768,1024]{1,0:T(8,128)}), f32[24,1024]{1,0:T(8,128)}) %reduce-scatter.8.cloned.1.call-update) | async-done | bytes 98320 | tf_op jit(solution)/shard_map/reduce_scatter | solution.py:462
  919.4 184.5 %reduce-scatter.10.cloned.1.call-done = f32[1,256,1024]{2,1,0:T(8,128)} async-done(((f32[1,4096,1024]{2,1,0:T(8,128)}), f32[1,256,1024]{2,1,0:T(8,128)}) %reduce-scatter.10.cloned.1.call-update) | async-done | bytes 1048592 | tf_op jit(solution)/shard_map/reduce_scatter | solution.py:453
  1103.9 187.6 %reduce-scatter.12.cloned.1.call-done = f32[1024,128]{1,0:T(8,128)} async-done(((f32[1024,4096]{1,0:T(8,128)}), f32[1024,128]{1,0:T(8,128)}) %reduce-scatter.12.cloned.1.call-update) | async-done | bytes 524304 | tf_op jit(solution)/shard_map/reduce_scatter | solution.py:459
  1291.5 187.2 %reduce-scatter.14.cloned.1.call-done = f32[128,1024]{1,0:T(8,128)} async-done(((f32[4096,1024]{1,0:T(8,128)}), f32[128,1024]{1,0:T(8,128)}) %reduce-scatter.14.cloned.1.call-update) | async-done | bytes 524304 | tf_op jit(solution)/shard_map/reduce_scatter | solution.py:461
  1478.7 1.6 copy.415
  (293 shorter events, 52.5 us)
Async XLA Ops:
  8.0 803.7 %reduce-scatter.16.cloned.1.call-start = ((), (), s32[]{:S(2)}) async-start(), calls=%async_computation.10 | async-start | bytes 2228224
  8.1 11.6 copy-start.4
  8.1 11.6 copy-start.16
  8.1 11.5 copy-start.31
  8.1 11.5 copy-start.43
  8.1 11.5 copy-start.72
  19.7 74.6 %copy-start.76 = (bf16[3,1024]{1,0:T(4,128)(2,1)S(1)}, bf16[3,1024]{1,0:T(4,128)(2,1)}, u32[]{:S(2)}) copy-start(bf16[3,1024]{1,0:T(4,128)(2,1)} %param.72) | copy-start | bytes 18436
  19.7 74.6 %copy-start.86 = (bf16[2,1024]{1,0:T(2,128)(2,1)S(1)}, bf16[2,1024]{1,0:T(2,128)(2,1)}, u32[]{:S(2)}) copy-start(bf16[2,1024]{1,0:T(2,128)(2,1)} %param.71) | copy-start | bytes 12292
  19.7 74.6 %copy-start.88 = (bf16[4096]{0:T(1024)(128)(2,1)S(1)}, bf16[4096]{0:T(1024)(128)(2,1)}, u32[]{:S(2)}) copy-start(bf16[4096]{0:T(1024)(128)(2,1)} %param.74) | copy-start | bytes 24580
  19.7 74.6 %copy-start.96 = (s32[2]{0:T(128)S(1)}, s32[2]{0:T(128)}, u32[]{:S(2)}) copy-start(s32[2]{0:T(128)} %param.65) | copy-start | bytes 28
  27.7 66.5 %collective-permute-start = (bf16[128,1024]{1,0:T(8,128)(2,1)}, bf16[128,1024]{1,0:T(8,128)(2,1)S(1)}, u32[]{:S(2)}, u32[]{:S(2)}) collective-permute-start(bf16[128,1024]{1,0:T(8,128)(2,1)} %get-tuple-element.498), channel_id=1, source_target_pairs={{0,16},{1,17},{2,18},{3,19},{4,20},{5,21},{6,22},{7,23},{8,24},{9,... | collective-permute-start | bytes 786440 | tf_op jit(solution)/shard_map/ppermute | solution.py:26
  94.3 116.6 %copy-start.77 = (bf16[3,1024]{1,0:T(4,128)(2,1)S(1)}, bf16[3,1024]{1,0:T(4,128)(2,1)}, u32[]{:S(2)}) copy-start(bf16[3,1024]{1,0:T(4,128)(2,1)} %param.72) | copy-start | bytes 18436
  113.2 29.7 %copy-start.35 = (bf16[128,1024]{0,1:T(8,128)(2,1)}, bf16[128,1024]{0,1:T(8,128)(2,1)S(1)}, u32[]{:S(2)}) copy-start(bf16[128,1024]{0,1:T(8,128)(2,1)S(1)} %copy.162) | copy-start | bytes 786436 | tf_op jit(solution)/shard_map/cond
  117.9 15.7 %slice-start.3 = ((s8[8388608]{0:T(1024)(128)(4,1)}), s8[4194304]{0:T(1024)(128)(4,1)S(1)}, s32[]{:S(2)}) async-start(s8[8388608]{0:T(1024)(128)(4,1)} %bitcast.571), calls=%async_computation.14 | async-start | bytes 8388608 | tf_op jit(solution)/shard_map/cond
  122.8 10.8 copy-start.20
  122.8 10.8 slice-start.4
  147.5 10.8 slice-start.9
  147.5 14.6 slice-start.11
  149.7 9.6 slice-start.10
  149.7 12.4 slice-start.12
  202.4 8.5 collective-permute-start.1
  210.9 128.6 %copy-start.5 = (bf16[768,1024]{1,0:T(8,128)(2,1)S(1)}, bf16[768,1024]{1,0:T(8,128)(2,1)}, u32[]{:S(2)}) copy-start(bf16[768,1024]{1,0:T(8,128)(2,1)} %param.67) | copy-start | bytes 4718596
  210.9 128.6 %copy-start.17 = (bf16[2,128,768]{2,1,0:T(8,128)(2,1)S(1)}, bf16[2,128,768]{2,1,0:T(8,128)(2,1)}, u32[]{:S(2)}) copy-start(bf16[2,128,768]{2,1,0:T(8,128)(2,1)} %param.63) | copy-start | bytes 1179652
  210.9 128.6 %copy-start.44 = (bf16[48,1024]{1,0:T(8,128)(2,1)S(1)}, bf16[48,1024]{1,0:T(8,128)(2,1)}, u32[]{:S(2)}) copy-start(bf16[48,1024]{1,0:T(8,128)(2,1)} %param.68) | copy-start | bytes 294916
  210.9 128.6 %copy-start.73 = (s32[2,48,128]{2,1,0:T(8,128)S(1)}, s32[2,48,128]{2,1,0:T(8,128)}, u32[]{:S(2)}) copy-start(s32[2,48,128]{2,1,0:T(8,128)} %param.64) | copy-start | bytes 147460
  211.0 12.1 copy-start.87
  211.0 12.1 copy-start.97
  236.6 15.5 %slice-start.5 = ((s8[8388608]{0:T(1024)(128)(4,1)}), s8[4194304]{0:T(1024)(128)(4,1)S(1)}, s32[]{:S(2)}) async-start(s8[8388608]{0:T(1024)(128)(4,1)} %bitcast.573), calls=%async_computation.16 | async-start | bytes 8388608 | tf_op jit(solution)/shard_map/cond
  241.5 10.5 copy-start.18
  241.5 10.6 slice-start.6
  272.6 15.5 %slice-start.7 = ((s8[8388608]{0:T(1024)(128)(4,1)}), s8[4194304]{0:T(1024)(128)(4,1)S(1)}, s32[]{:S(2)}) async-start(s8[8388608]{0:T(1024)(128)(4,1)} %bitcast.587), calls=%async_computation.18 | async-start | bytes 8388608 | tf_op jit(solution)/shard_map/cond
  274.7 13.3 copy-start.83
  274.7 13.3 slice-start.8
  293.7 14.4 copy-start.19
  293.7 14.4 copy-start.50
  293.7 28.1 %slice-start.13 = ((s8[8388608]{0:T(1024)(128)(4,1)}), s8[4194304]{0:T(1024)(128)(4,1)S(1)}, s32[]{:S(2)}) async-start(s8[8388608]{0:T(1024)(128)(4,1)} %bitcast.766), calls=%async_computation.24 | async-start | bytes 8388608 | tf_op jit(solution)/shard_map/cond
  308.1 13.7 copy-start.94
  308.1 13.7 slice-start.14
  328.5 11.0 copy-start.74
  328.5 11.0 collective-permute-start.2
  339.5 9.7 copy-start.32
  352.1 535.2 %all-reduce.6.cloned.1.call-start = ((), (), s32[]{:S(2)}) async-start(), calls=%async_computation.6 | async-start | bytes 393216 | tf_op jit(solution)/shard_map/psum | solution.py:464
  352.7 566.7 %reduce-scatter.8.cloned.1.call-start = ((), (), s32[]{:S(2)}) async-start(), calls=%async_computation.5 | async-start | bytes 3244032 | tf_op jit(solution)/shard_map/reduce_scatter | solution.py:462
  353.5 750.4 %reduce-scatter.10.cloned.1.call-start = ((), (), s32[]{:S(2)}) async-start(), calls=%async_computation.7 | async-start | bytes 17825792 | tf_op jit(solution)/shard_map/reduce_scatter | solution.py:453
  354.2 937.3 %reduce-scatter.12.cloned.1.call-start = ((), (), s32[]{:S(2)}) async-start(), calls=%async_computation.8 | async-start | bytes 17301504 | tf_op jit(solution)/shard_map/reduce_scatter | solution.py:459
  354.8 1123.9 %reduce-scatter.14.cloned.1.call-start = ((), (), s32[]{:S(2)}) async-start(), calls=%async_computation.9 | async-start | bytes 17301504 | tf_op jit(solution)/shard_map/reduce_scatter | solution.py:461
  354.9 458.4 %copy-start.30 = (f32[2,128,384]{2,1,0:T(8,128)S(1)}, f32[2,128,384]{2,1,0:T(8,128)}, u32[]{:S(2)}) copy-start(f32[2,128,384]{2,1,0:T(8,128)} %copy-done.29) | copy-start | bytes 1179652
  356.4 456.8 %collective-permute-start.3 = (bf16[2,128,384]{2,1,0:T(8,128)(2,1)S(1)}, bf16[2,128,384]{2,1,0:T(8,128)(2,1)S(1)}, u32[]{:S(2)}, u32[]{:S(2)}) collective-permute-start(bf16[2,128,384]{2,1,0:T(8,128)(2,1)S(1)} %slice.837), channel_id=1, source_target_pairs={{0,16},{1,17},{2,18},{3,19},{4,20},{5,21},{6,22},{7,23},{8,24},{9,... | collective-permute-start | bytes 589832 | tf_op jit(solution)/shard_map/ppermute | solution.py:26
  (45 other events, 140.5 us)
Sparse Core Ops, SparseCore 0:
  352.2 459.3 reduce-scatter.15
  818.5 100.7 reduce-scatter.7
  924.6 179.1 reduce-scatter.9
  1106.7 184.7 reduce-scatter.11
  1294.3 184.3 reduce-scatter.13
Sparse Core Ops, SparseCore 1:
  359.6 527.7 all-reduce.5
where the time goes:
time: 1500 us; the launch traced here: 1490 us
  waiting for transfers between devices  762 us (51%)
  blocking collectives  441 us (29%)
  matrix products  147 us (10%)
  local copies, waits for them, and re-layouts  60.6 us (4%)
  loops' own time  28.7 us (2%)
  other arithmetic  27.6 us (2%)
  between operations  15.8 us (1%)
    psum x1, blocking collectives, shards(): lax.psum((carried['var'], carried['gains'], carried['shifts']), ('section...  441 us
    reduce_scatter x1, waiting for transfers between devices, shards(): lax.psum_scatter(carried['w_in'], ('section', 'dp'), scatter_dimension=1,...  188 us
    reduce_scatter x1, waiting for transfers between devices, shards(): lax.psum_scatter(carried['w_out'], ('section', 'dp'), scatter_dimension=0...  187 us
    reduce_scatter x1, waiting for transfers between devices, shards(): lax.psum_scatter(carried['attn'].reshape(1, 4 * D, D), 'dp', scatter_dime...  184 us
    ppermute x4, waiting for transfers between devices, from_behind(): lax.ppermute(value, axis, [(source, source + steps) for source in range(l...  82 us
    psum x1, waiting for transfers between devices, shards(): lax.psum((carried['var'], carried['gains'], carried['shifts']), ('section...  73.4 us
    dot_general x12, matrix products, matmul_tn(): lax.dot_general(left_side, right_side, (((0,), (0,)), ((), ())), preferre...  57.5 us
    dot_general x12, matrix products, matmul(): return jnp.dot(left_side, right_side, preferred_element_type=jnp.float32)  39.5 us
  transfers between devices with their start and end apart: 10, of which 9 were waited for; matrix products, arithmetic and copies ran while one was open for 0% of the time, Pallas kernels for 0%

commit v1 on v0

--- a/solution.py
+++ b/solution.py
@@ -1,6 +1,10 @@
+import functools
+
 import jax
 import jax.numpy as jnp
 from jax import lax
+from jax.experimental import pallas as pl
+from jax.experimental.pallas import tpu as pltpu
 from jax.sharding import PartitionSpec as P
 
 D = 1024
@@ -483,6 +487,1183 @@
     )
 
 
+F32 = jnp.float32
+BF = jnp.bfloat16
+I32 = jnp.int32
+MESH = pl.DeviceIdType.MESH
+CELLS = 256
+SLOT = 64
+WIDE = 1152
+LANES = 128
+SCALE = 0.125
+ROOT_HALF = 0.7071067811865476
+ROOT_TAU = 0.3989422804014327
+
+
+def nn(a, b):
+    return jnp.dot(a, b, preferred_element_type=F32)
+
+
+def nt(a, b):
+    return lax.dot_general(a, b, (((1,), (1,)), ((), ())), preferred_element_type=F32)
+
+
+def tn(a, b):
+    return lax.dot_general(a, b, (((0,), (0,)), ((), ())), preferred_element_type=F32)
+
+
+def at(start, size):
+    if isinstance(start, int):
+        return pl.ds(start, size)
+    return pl.ds(pl.multiple_of(start, size), size)
+
+
+def each(count, body):
+    def step(index, carry):
+        body(index)
+        return carry
+
+    lax.fori_loop(0, count, step, 0)
+
+
+def iota(shape, dim):
+    return lax.broadcasted_iota(I32, shape, dim)
+
+
+def halves(value):
+    high = value.astype(BF)
+    return high, (value - high.astype(F32)).astype(BF)
+
+
+def pixel_column(slot):
+    return ((slot & (SLOT - 1)) << 4) + (slot >> 6)
+
+
+def slot_tile(index, rows, columns):
+    match = pixel_column(iota((rows, 1), 0) + index * rows)
+    return jnp.where(iota((rows, columns), 1) == match, 1.0, 0.0).astype(BF)
+
+
+def spread(tile):
+    return jnp.concatenate([tile] * (WIDE // LANES), axis=1)
+
+
+def front_tables(r):
+    def place(index):
+        tile = slot_tile(index, 256, V * PIX)
+        r.table[at(index * 256, 256), :] = nn(tile, r.raw[...]).astype(BF)
+        r.pat[:, at(index * 256, 256)] = nt(r.pix[...], tile).astype(BF)
+
+    each(4, place)
+    r.table[1024:1072, :] = r.embed[...]
+    r.table[1072:WIDE, :] = jnp.zeros((WIDE - 1072, D), BF)
+    lane = iota((CELLS, LANES), 1)
+    r.pat[:, 1024:WIDE] = jnp.where(lane < V, 1.0, 0.0).astype(BF)
+    twice = jnp.where(iota((V, LANES), 1) & (SLOT - 1) == iota((V, LANES), 0), 1.0, 0.0).astype(BF)
+    for sample in range(2):
+        present = tn(r.masks[sample].astype(F32).astype(BF), twice)
+        r.keep[sample * 128 : sample * 128 + 128, :] = present
+
+
+def front_query(r):
+    first = jnp.broadcast_to(r.vecs[0:1, :], (16, D))
+    query = nn(first, r.attn[0])[0:1, :] + r.vecs[1:2, :].astype(F32)
+    own = iota((HEADS, D), 1) >> 6 == iota((HEADS, D), 0)
+    high, low = halves(jnp.where(own, jnp.broadcast_to(query, (HEADS, D)), 0.0))
+    r.qhead[0:HEADS, :] = high
+    r.qhead[HEADS : 2 * HEADS, :] = low
+    both = nt(r.qhead[...], r.attn[1])
+    folded = (both[0:HEADS] + both[HEADS : 2 * HEADS]).astype(BF)
+    r.fold[...] = folded
+    r.score[...] = nt(folded, r.table[...]) * SCALE
+
+
+def front_values(r):
+    def tile(index):
+        lanes = at(index * 256, 256)
+        r.mid[:, lanes] = nn(r.table[...], r.attn[2, :, lanes]).astype(BF)
+
+    each(4, tile)
+
+
+def front_scores(r, head):
+    row = r.score[pl.ds(head, 1), :]
+    total = None
+    for k in range(WIDE // LANES):
+        part = r.pat[:, k * LANES : (k + 1) * LANES].astype(F32) * row[:, k * LANES : (k + 1) * LANES]
+        total = part if total is None else total + part
+    total = total + pltpu.roll(total, SLOT, 1)
+    total = jnp.where(r.keep[...] > 0.5, total, MASKED)
+    top = jnp.max(total, axis=1, keepdims=True)
+    grown = jnp.exp(total - top)
+    return grown / (0.5 * jnp.sum(grown, axis=1, keepdims=True))
+
+
+def front_forward(r, out):
+    first_half = iota((CELLS, LANES), 1) < HEAD
+
+    def pair(index):
+        lanes = at(index * LANES, LANES)
+        found = []
+        for part in range(2):
+            head = index * 2 + part
+            weights = front_scores(r, head)
+            r.probs[at(head * 2, 2)] = weights.reshape(2, 128, LANES)
+            pooled = r.pat[...] * spread(weights.astype(BF))
+            found.append(nn(pooled, r.mid[:, lanes]))
+        values = jnp.where(first_half, found[0], found[1]) + r.vecs[2:3, lanes].astype(F32)
+        r.agg[:, lanes] = values.astype(BF)
+
+    each(HEADS // 2, pair)
+
+    def tile(index):
+        lanes = at(index * 256, 256)
+        out[:, lanes] = (nn(r.agg[...], r.attn[3, :, lanes]) + r.vecs[3:4, lanes].astype(F32)).astype(BF)
+
+    each(4, tile)
+
+
+def front_back_values(r, d_out):
+    def tile(index):
+        rows = at(index * 256, 256)
+        grad = nt(d_out[...], r.attn[3, rows, :])
+        r.small[64:65, rows] = jnp.sum(grad, axis=0, keepdims=True)
+        r.small[65:66, rows] = jnp.sum(d_out[:, rows].astype(F32), axis=0, keepdims=True)
+        r.dlow[:, rows] = grad.astype(BF)
+
+    each(4, tile)
+    r.turn_a[...] = r.dlow[...].T
+
+
+def front_back_heads(r):
+    first_half = iota((CELLS, LANES), 1) < HEAD
+    r.input_sum[...] = jnp.zeros((CELLS, D), F32)
+
+    def pair(index):
+        lanes = at(index * LANES, LANES)
+        grads = r.dlow[:, lanes]
+        mid = r.mid[:, lanes]
+        for part in range(2):
+            head = index * 2 + part
+            mine = first_half if part == 0 else jnp.logical_not(first_half)
+            own = jnp.where(mine, grads, jnp.zeros_like(grads))
+            weights = r.probs[at(head * 2, 2)].reshape(CELLS, LANES)
+            low = weights.astype(BF)
+            lowf = low.astype(F32)
+            total = None
+            for k in range(WIDE // 384):
+                wide = nt(own, mid[k * 384 : (k + 1) * 384, :])
+                for j in range(3):
+                    n = k * 3 + j
+                    cols = slice(n * LANES, (n + 1) * LANES)
+                    piece = wide[:, j * LANES : (j + 1) * LANES]
+                    term = piece * r.pat[:, cols].astype(F32)
+                    total = term if total is None else total + term
+                    if n < 8:
+                        r.input_sum[:, cols] = r.input_sum[:, cols] + lowf * piece
+            total = total + pltpu.roll(total, SLOT, 1)
+            inner = 0.5 * jnp.sum(weights * total, axis=1, keepdims=True)
+            d_score = (weights * (total - inner)).astype(BF).astype(F32)
+            row = r.score[pl.ds(head, 1), :]
+            for n in range(9):
+                cols = slice(n * LANES, (n + 1) * LANES)
+                if n < 8:
+                    r.input_sum[:, cols] = r.input_sum[:, cols] + d_score * row[:, cols]
+                r.uses[head, :, cols] = SCALE * jnp.sum(
+                    d_score * r.pat[:, cols].astype(F32), axis=0, keepdims=True
+                )
+            pooled = r.pat[...] * spread(low)
+            r.turned[at(head * HEAD, HEAD), :] = nn(r.turn_a[at(head * HEAD, HEAD), :], pooled).astype(BF)
+
+    each(HEADS // 2, pair)
+
+
+def put_front(r, which, quarter, value):
+    y, c = quarter // 2, quarter % 2
+    for j in range(2):
+        r.grads[which * 2 + j, at((c * 2 + y) * 128, 128), :] = value[j * 128 : (j + 1) * 128].astype(BF)
+
+
+def front_back_out(r, d_out):
+    r.turn_b[...] = r.agg[...].T
+
+    def tile(index):
+        put_front(r, 1, index, nn(r.turn_b[at(index * 256, 256), :], d_out[...]))
+
+    each(4, tile)
+
+
+def front_back_table(r):
+    uses = jnp.concatenate([r.uses[h] for h in range(HEADS)], axis=0).astype(BF)
+    r.small[48:64, :] = nn(uses, r.table[...])
+    r.mid[...] = r.turned[...].T
+
+
+def front_back_projection(r):
+    def values(index):
+        rows = at(index * 256, 256)
+        put_front(r, 0, index, tn(r.table[:, rows], r.mid[...]))
+
+    each(4, values)
+
+
+def front_back_pixels(r):
+    uses = jnp.concatenate([r.uses[h] for h in range(HEADS)], axis=0).astype(BF)
+
+    def pixels(index):
+        lanes = at(index * 256, 256)
+        full = nt(r.mid[...], r.attn[2, lanes, :]) + tn(uses, r.fold[:, lanes])
+        r.turned[:, lanes] = full[0:1024].astype(BF)
+        r.small[0:48, lanes] = full[1024:1072]
+
+    each(4, pixels)
+
+
+def front_back_order(r):
+    def order(index):
+        row = iota((256, 1), 0) + index * 256
+        piece, k = row // 48, row % 48
+        owner = ((piece & 1) * 2 + ((piece >> 1) & 1)) * 4 + ((piece >> 2) & 1) * 2 + (piece >> 3)
+        natural = owner * 24 + jnp.where(k < 24, k, k + 360)
+        slot = (natural & (PIX - 1)) * SLOT + (natural >> 4)
+        pick = jnp.where(iota((256, D), 1) == slot, 1.0, 0.0).astype(BF)
+        r.patch_sum[at(index * 256, 256), :] = nn(pick, r.turned[:, 0:1024]).astype(BF)
+
+    each(3, order)
+
+
+def front_back_inputs(r, own_half, other_half):
+    low = r.input_sum[...].astype(BF)
+    r.dlow[...] = low
+    for half, out in ((0, own_half), (1, other_half)):
+        column = pixel_column(iota((D, 1), 0)) - half * 384
+        pick = jnp.where(iota((D, 384), 1) == column, 1.0, 0.0).astype(BF)
+        out[...] = nn(r.dlow[...], pick).astype(out.dtype)
+
+
+def row_mean(x):
+    return jnp.mean(x, axis=1, keepdims=True)
+
+
+def col_sum(x):
+    return jnp.sum(x, axis=0, keepdims=True)
+
+
+def trunk_ahead(r):
+    def tile(index):
+        n, k = index // 4, index % 4
+        rows = at(k * 256, 256)
+        r.grads[n, 0:256, rows] = nt(r.cot[...], r.bufs[1, n, rows, :]).astype(BF)
+
+    each(16, tile)
+    r.small[3:4, :] = col_sum(r.cot[...].astype(F32))
+
+
+def normalise(r, source, spread_rows, unit, gain, shift, out):
+    def rows_of(index):
+        rows = at(index * 64, 64)
+        x = source[rows, :]
+        centred = x - row_mean(x)
+        rstd = lax.rsqrt(row_mean(centred * centred) + EPSILON)
+        scaled = centred * rstd
+        unit[rows, :] = scaled
+        spread_rows[rows, :] = jnp.broadcast_to(rstd, (64, LANES))
+        out[rows, :] = (scaled * gain + shift).astype(BF)
+
+    each(4, rows_of)
+
+
+def trunk_attention(r, front):
+    shift_rows = r.shifts[...].astype(F32)
+    gain_rows = r.gains[...].astype(F32)
+
+    def enter(index):
+        rows = at(index * 128, 128)
+        lead = r.leads[index].astype(F32) / 100.0
+        r.resid[rows, :] = front[rows, :].astype(F32) + lead * shift_rows[2:3]
+
+    each(2, enter)
+    normalise(r, r.resid, r.rstd_one, r.unit_one, gain_rows[0:1], shift_rows[0:1], r.normed)
+
+    def project(index):
+        lanes = at(index * 256, 256)
+        x = r.normed[...]
+        r.q[:, lanes] = (nn(x, r.attn[0, :, lanes]) + r.vecs[0:1, lanes].astype(F32)).astype(BF)
+        r.k[:, lanes] = nn(x, r.attn[1, :, lanes]).astype(BF)
+        r.v[:, lanes] = (nn(x, r.attn[2, :, lanes]) + r.vecs[1:2, lanes].astype(F32)).astype(BF)
+
+    each(4, project)
+    first = iota((128, LANES), 1) < HEAD
+
+    def pair(index):
+        sample, hp = index // 8, index % 8
+        rows, lanes = at(sample * 128, 128), at(hp * LANES, LANES)
+        q, k, v = r.q[rows, lanes], r.k[rows, lanes], r.v[rows, lanes]
+        none = jnp.zeros_like(q)
+        mixed = None
+        for part in range(2):
+            mine = first if part == 0 else jnp.logical_not(first)
+            scores = nt(jnp.where(mine, q, none), k) * SCALE
+            grown = jnp.exp(scores - jnp.max(scores, axis=1, keepdims=True))
+            probs = grown / jnp.sum(grown, axis=1, keepdims=True)
+            r.probs[index * 2 + part] = probs
+            term = nn(probs.astype(BF), jnp.where(mine, v, none))
+            mixed = term if mixed is None else mixed + term
+        r.mixed[rows, lanes] = mixed.astype(BF)
+
+    each(16, pair)
+
+    def leave(index):
+        lanes = at(index * 256, 256)
+        grown = nn(r.mixed[...], r.attn[3, :, lanes]) + r.vecs[2:3, lanes].astype(F32)
+        r.resid[:, lanes] = r.resid[:, lanes] + grown
+
+    each(4, leave)
+    normalise(r, r.resid, r.rstd_two, r.unit_two, gain_rows[1:2], shift_rows[1:2], r.second)
+
+
+def curve(x):
+    area = 0.5 + 0.5 * lax.erf(x * ROOT_HALF)
+    return x * area, area + x * (ROOT_TAU * jnp.exp(-0.5 * x * x))
+
+
+def trunk_hidden(r):
+    def tile(index):
+        n, k = index // 4, index % 4
+        lanes = at(k * 256, 256)
+        pre = nn(r.second[...], r.bufs[0, n, :, lanes]) + r.bias[n, :, lanes].astype(F32)
+        value, slope = curve(pre)
+        r.grads[n, 256:512, lanes] = value.astype(BF)
+        r.grads[n, 0:256, lanes] = (r.grads[n, 0:256, lanes].astype(F32) * slope).astype(BF)
+
+    each(16, tile)
+
+    def back(index):
+        rows = at(index * 256, 256)
+        total = None
+        for n in range(4):
+            term = nt(r.grads[n, 0:256, :], r.bufs[0, n, rows, :])
+            total = term if total is None else total + term
+        r.d_mid[:, rows] = total
+
+    each(4, back)
+
+
+def norm_back(grad, unit, rstd, gain):
+    scaled = grad * gain
+    along = row_mean(scaled * unit)
+    return rstd * (scaled - row_mean(scaled) - unit * along)
+
+
+def trunk_back(r, d_in):
+    gain_rows = r.gains[...].astype(F32)
+    shift_rows = r.shifts[...].astype(F32)
+    r.small[2:3, :] = jnp.zeros((1, D), F32)
+    r.small[4:9, :] = jnp.zeros((5, D), F32)
+
+    def second(index):
+        rows = at(index * 64, 64)
+        grad, unit = r.d_mid[rows, :], r.unit_two[rows, :]
+        mid = r.cot[rows, :].astype(F32) + norm_back(grad, unit, r.rstd_two[rows, 0:1], gain_rows[1:2])
+        r.d_mid[rows, :] = mid
+        r.d_low[rows, :] = mid.astype(BF)
+        r.small[2:3, :] += col_sum(mid)
+        r.small[5:6, :] += col_sum(grad * unit)
+        r.small[7:8, :] += col_sum(grad)
+
+    each(4, second)
+
+    def mix(index):
+        rows = at(index * 256, 256)
+        r.second[:, rows] = nt(r.d_low[...], r.attn[3, rows, :]).astype(BF)
+
+    each(4, mix)
+    first = iota((128, LANES), 1) < HEAD
+    r.small[0:2, :] = jnp.zeros((2, D), F32)
+
+    def pair(index):
+        sample, hp = index // 8, index % 8
+        rows, lanes = at(sample * 128, 128), at(hp * LANES, LANES)
+        q, k, v = r.q[rows, lanes], r.k[rows, lanes], r.v[rows, lanes]
+        d_mixed = r.second[rows, lanes]
+        none = jnp.zeros_like(q)
+        d_q = d_k = d_v = None
+        for part in range(2):
+            mine = first if part == 0 else jnp.logical_not(first)
+            own = jnp.where(mine, d_mixed, none)
+            probs = r.probs[index * 2 + part]
+            d_probs = nt(own, v)
+            inner = jnp.sum(probs * d_probs, axis=1, keepdims=True)
+            d_scores = (probs * (d_probs - inner)).astype(BF)
+            terms = (
+                nn(d_scores, jnp.where(mine, k, none)),
+                tn(d_scores, jnp.where(mine, q, none)),
+                tn(probs.astype(BF), own),
+            )
+            d_q = terms[0] if d_q is None else d_q + terms[0]
+            d_k = terms[1] if d_k is None else d_k + terms[1]
+            d_v = terms[2] if d_v is None else d_v + terms[2]
+        d_q = d_q * SCALE
+        r.q[rows, lanes] = d_q.astype(BF)
+        r.k[rows, lanes] = (d_k * SCALE).astype(BF)
+        r.v[rows, lanes] = d_v.astype(BF)
+        r.small[0:1, lanes] += col_sum(d_q)
+        r.small[1:2, lanes] += col_sum(d_v)
+
+    each(16, pair)
+
+    def inward(index):
+        rows = at(index * 256, 256)
+        total = nt(r.q[...], r.attn[0, rows, :]) + nt(r.k[...], r.attn[1, rows, :])
+        r.unit_two[:, rows] = total + nt(r.v[...], r.attn[2, rows, :])
+
+    each(4, inward)
+
+    def start(index):
+        rows = at(index * 64, 64)
+        grad, unit = r.unit_two[rows, :], r.unit_one[rows, :]
+        whole = r.d_mid[rows, :] + norm_back(grad, unit, r.rstd_one[rows, 0:1], gain_rows[0:1])
+        d_in[rows, :] = whole.astype(BF)
+        lead = r.leads[index // 2].astype(F32) / 100.0
+        r.small[4:5, :] += col_sum(grad * unit)
+        r.small[6:7, :] += col_sum(grad)
+        r.small[8:9, :] += lead * col_sum(whole)
+
+    each(4, start)
+
+
+def trunk_out(r, out):
+    def tile(index):
+        lanes = at(index * 256, 256)
+        total = r.resid[:, lanes] + r.vecs[3:4, lanes].astype(F32)
+        for n in range(4):
+            total = total + nn(r.grads[n, 256:512, :], r.bufs[1, n, :, lanes])
+        out[:, lanes] = total.astype(BF)
+
+    each(4, tile)
+
+
+def trunk_weights(r):
+    r.turn_a[...] = r.normed[...].T
+    r.turn_b[...] = r.mixed[...].T
+
+    def quarter(index):
+        y, c = index // 2, index % 2
+        rows = at(index * 256, 256)
+        for m, (left, right) in enumerate(
+            ((r.turn_a, r.q), (r.turn_a, r.k), (r.turn_a, r.v), (r.turn_b, r.d_low))
+        ):
+            value = nn(left[rows, :], right[...])
+            for j in range(4):
+                spot = ((c * 2 + y) * 4 + (m % 2) * 2 + m // 2) * 64
+                r.bufs[0, j, at(spot, 64), :] = value[j * 64 : (j + 1) * 64].astype(BF)
+
+    each(4, quarter)
+
+
+def hidden_tables(r):
+    r.win_t[...] = r.win[...].T
+    r.units[...] = jnp.broadcast_to(r.unit_bias[0:1, :].astype(F32), (256, 256)).T
+    r.unit_two[...] = jnp.zeros((256, D), F32)
+    r.d_mid[...] = jnp.zeros((256, D), F32)
+    r.bias_sum[...] = jnp.zeros((256, 256), F32)
+
+
+def hidden_plane(r, plane):
+    def tile(index):
+        rows = at(index * 256, 256)
+        x, cot = r.bufs[0, plane, rows, :], r.bufs[1, plane, rows, :]
+        value, slope = curve(nt(r.win_t[...], x) + r.units[...])
+        grad = nt(r.wout[...], cot) * slope
+        r.bias_sum[...] += grad
+        r.unit_two[...] += nn(grad.astype(BF), x)
+        r.d_mid[...] += nn(value.astype(BF), cot)
+
+    each(4, tile)
+
+
+def remote(source, target, sent, arrived, device):
+    return pltpu.make_async_remote_copy(
+        src_ref=source,
+        dst_ref=target,
+        send_sem=sent,
+        recv_sem=arrived,
+        device_id=device,
+        device_id_type=MESH,
+    )
+
+
+class Place:
+    def __init__(self):
+        self.section = lax.axis_index("section")
+        self.me = lax.axis_index("dp")
+        self.c = self.me % 2
+        self.y = (self.me // 2) % 2
+        self.low = (self.me // 4) % 2
+        self.high = self.me // 8
+        self.across = {"section": 1 - self.section}
+        self.core = {"dp": self.me + 1 - 2 * self.c}
+        self.beside = {"dp": self.me + 2 - 4 * self.y}
+        self.near = {"dp": self.me + 4 - 8 * self.low}
+        self.far = {"dp": self.me + 8 - 16 * self.high}
+        self.both = {"dp": self.me + 12 - 8 * self.low - 16 * self.high}
+
+    def plane(self, step):
+        low = (self.low + step % 2) % 2
+        high = (self.high + step // 2) % 2
+        return high * 2 + low
+
+    def levels(self):
+        return (self.core, self.beside, self.near, self.far)
+
+
+class Share:
+    def __init__(self, r, place, which, sent, arrived):
+        self.place, self.sent, self.arrived = place, sent, arrived
+        self.buf = r.bufs.at[which]
+        self.pair = place.y * 2 + place.c
+        self.other = (1 - place.y) * 2 + place.c
+        self.mine = place.high * 2 + place.low
+
+    def copy(self, plane, spot, number, device):
+        block = self.buf.at[plane, at(spot * 256, 256)]
+        return remote(block, block, self.sent.at[number], self.arrived.at[plane * 4 + spot], device)
+
+    def wait(self, plane, spot):
+        self.copy(plane, spot, 0, self.place.core).wait_recv()
+
+    def along(self, plane, number, to_upper):
+        step = 4 if to_upper else -4
+        device = {"dp": self.place.me + step}
+        pl.when(self.mine < 3 if to_upper else self.mine > 0)(
+            lambda: self.copy(plane, self.pair, number, device).start()
+        )
+
+    def open(self):
+        self.along(self.mine, 0, True)
+        self.along(self.mine, 1, False)
+        self.copy(self.mine, self.pair, 2 + self.mine, self.place.beside).start()
+        self.copy(self.mine, self.pair, 6 + self.mine, self.place.core).start()
+
+    def pass_on(self, distance):
+        for below in (True, False):
+            plane = self.mine - distance if below else self.mine + distance
+
+            @pl.when(plane >= 0 if below else plane < 4)
+            def _():
+                self.wait(plane, self.pair)
+                self.along(plane, 14 + plane, below)
+                self.copy(plane, self.pair, 2 + plane, self.place.beside).start()
+                self.copy(plane, self.pair, 6 + plane, self.place.core).start()
+
+            if distance == 1 and not below:
+                continue
+            before = plane + 1 if below else plane - 1
+
+            @pl.when(before >= 0 if below else before < 4)
+            def _():
+                self.wait(before, self.other)
+                self.copy(before, self.other, 10 + before, self.place.core).start()
+
+    def settle(self, plane):
+        self.wait(plane, self.place.y * 2 + 1 - self.place.c)
+        self.wait(plane, (1 - self.place.y) * 2 + 1 - self.place.c)
+
+    def close(self):
+        def done(number):
+            self.copy(0, 0, number, self.place.core).wait_send()
+
+        pl.when(self.mine < 3)(lambda: done(0))
+        pl.when(self.mine > 0)(lambda: done(1))
+        for number in range(2, 14):
+            done(number)
+        for plane in range(4):
+            gone = ((plane < self.mine) & (self.mine < 3)) | ((plane > self.mine) & (self.mine > 0))
+            pl.when(gone)(functools.partial(done, 14 + plane))
+
+
+class Halving:
+    def __init__(self, place, source, room, sizes, sent, arrived, done, target=None):
+        self.place, self.source, self.room, self.sizes = place, source, room, sizes
+        self.sent, self.arrived, self.done, self.target = sent, arrived, done, target
+        self.bits = (place.c, place.y, place.low, place.high)
+
+    def takes(self, level):
+        if self.target is None or level < 2:
+            return None
+        on_low = self.place.low == self.target[0]
+        return on_low if level == 2 else on_low & (self.place.high == self.target[1])
+
+    def gives(self, level):
+        if self.target is None or level < 2:
+            return None
+        on_low = self.place.low == self.target[0]
+        return jnp.logical_not(on_low) if level == 2 else on_low & (self.place.high != self.target[1])
+
+    def when(self, condition, action):
+        if condition is None:
+            action()
+        else:
+            pl.when(condition)(action)
+
+    def part(self, j, level, side):
+        rows = self.sizes[level]
+        start = 0 if self.target is not None and level >= 2 else side * rows
+        return self.source(j, start, rows) if level == 0 else self.room(j, level - 1, start, rows)
+
+    def copy(self, j, level):
+        give = self.part(j, level, 1 - self.bits[level])
+        target = self.room(j, level, 0, self.sizes[level])
+        device = self.place.levels()[level]
+        return remote(give, target, self.sent.at[j, level], self.arrived.at[j, level], device)
+
+    def begin(self, j, level):
+        self.when(self.gives(level), lambda: self.copy(j, level).start())
+
+    def finish(self, j, level):
+        self.when(self.takes(level), lambda: self.take(j, level))
+        if level < 3:
+            self.begin(j, level + 1)
+
+    def take(self, j, level):
+        self.copy(j, level).wait_recv()
+        mine = self.part(j, level, self.bits[level])
+        room = self.room(j, level, 0, self.sizes[level])
+        total = mine[...].astype(F32) + room[...].astype(F32)
+        if level == 3:
+            self.done(j, total)
+        else:
+            room[...] = total.astype(BF)
+
+    def close(self, j):
+        for level in range(4):
+            self.when(self.gives(level), lambda: self.copy(j, level).wait_send())
+
+
+class Doubling:
+    def __init__(self, r, place, rows, sent, arrived):
+        self.r, self.place, self.rows, self.sent, self.arrived = r, place, rows, sent, arrived
+
+    def before(self, level):
+        return self.r.small.at[0 : self.rows] if level == 0 else self.r.small_in.at[level - 1, 0 : self.rows]
+
+    def copy(self, level):
+        target = self.r.small_in.at[level, 0 : self.rows]
+        device = self.place.levels()[level]
+        return remote(self.before(level), target, self.sent.at[level], self.arrived.at[level], device)
+
+    def begin(self):
+        self.copy(0).start()
+
+    def finish(self, level):
+        self.copy(level).wait_recv()
+        rows = slice(0, self.rows)
+        self.r.small_in[level, rows] = self.before(level)[...] + self.r.small_in[level, rows]
+        if level < 3:
+            self.copy(level + 1).start()
+
+    def close(self):
+        for level in range(4):
+            self.copy(level).wait_send()
+
+
+def greet(place):
+    barrier = pltpu.get_barrier_semaphore()
+    devices = (place.across, place.core, place.beside, place.near, place.far, place.both)
+    for device in devices:
+        pl.semaphore_signal(barrier, inc=1, device_id=device, device_id_type=MESH)
+    pl.semaphore_wait(barrier, len(devices))
+
+
+def across(r, place, number, source, target):
+    return remote(source, target, r.over_sent.at[number], r.over_come.at[number], place.across)
+
+
+def front_tail(r, place):
+    own = at((place.y * 2 + place.c) * 256, 256)
+    high, low = halves(r.small_in[3, 48:64])
+    r.fold_sum[0:16, :] = high
+    r.fold_sum[16:32, :] = low
+    both = nn(r.fold_sum[...], r.attn[1])
+    mine = iota((HEADS, D), 1) >> 6 == iota((HEADS, D), 0)
+    query = col_sum(jnp.where(mine, both[0:HEADS] + both[HEADS : 2 * HEADS], 0.0))
+    r.query_row[0:1, :] = query
+    high, low = halves(query)
+    row = iota((16, D), 0)
+    pair = jnp.where(row == 0, high.astype(F32), jnp.where(row == 1, low.astype(F32), 0.0))
+    r.query_pair[...] = pair.astype(BF)
+
+    @pl.when(place.high + place.low == 0)
+    def _():
+        first = jnp.broadcast_to(r.vecs[0:1, own].astype(F32), (16, 256))
+        first = jnp.where(iota((16, 256), 0) < 2, first, 0.0).astype(BF)
+        r.attn_out[...] = tn(first, r.query_pair[...])
+        r.vec_out[...] = col_sum(nt(r.query_pair[...], r.attn[0, own, :]))
+
+    @pl.when((place.high == 0) & (place.low == 1))
+    def _():
+        left = jnp.concatenate([r.fold_sum[0:16, own], r.fold_sum[16:32, own], r.fold_sum[0:16, own]], axis=0)
+        right = jnp.concatenate([r.qhead[0:16, :], r.qhead[0:16, :], r.qhead[16:32, :]], axis=0)
+        r.attn_out[...] = tn(left, right)
+        r.vec_out[...] = r.query_row[0:1, own]
+
+    @pl.when(place.high == 1)
+    def _():
+        r.vec_out[...] = r.small_in[3, pl.ds(64 + place.low, 1), own]
+
+
+def front_section(r, place):
+    def load(number, source, target):
+        return pltpu.make_async_copy(source, target, r.loads.at[number])
+
+    mine = place.me * 128
+    half = FF // 2
+    loads = [
+        load(0, r.patches_in.at[0], r.pix.at[0:128]),
+        load(1, r.patches_in.at[1], r.pix.at[128:256]),
+        load(2, r.weight_in, r.raw),
+        load(3, r.attn_in.at[0, 0], r.attn.at[0]),
+        load(4, r.attn_in.at[0, 1], r.attn.at[1]),
+        load(5, r.attn_in.at[0, 2], r.attn.at[2]),
+        load(6, r.attn_in.at[0, 3], r.attn.at[3]),
+        load(7, r.cot_in.at[0], r.bufs.at[1, place.plane(0), at((place.y * 2 + place.c) * 256, 128)]),
+        load(8, r.cot_in.at[1], r.bufs.at[1, place.plane(0), at((place.y * 2 + place.c) * 256 + 128, 128)]),
+        load(9, r.mlp_in.at[:, at(mine, 128)], r.win.at[:, 0:128]),
+        load(10, r.mlp_in.at[:, at(half + mine, 128)], r.win.at[:, 128:256]),
+        load(11, r.mlp_out.at[at(mine, 128), :], r.wout.at[0:128]),
+        load(12, r.mlp_out.at[at(half + mine, 128), :], r.wout.at[128:256]),
+    ]
+    for one in loads:
+        one.start()
+    cots = Share(r, place, 1, r.cot_sent, r.cot_come)
+    hiddens = Share(r, place, 0, r.x_sent, r.x_come)
+    greet(place)
+    for one in loads[0:3]:
+        one.wait()
+    front_tables(r)
+    loads[7].wait()
+    loads[8].wait()
+    cots.open()
+    loads[3].wait()
+    loads[4].wait()
+    front_query(r)
+    loads[5].wait()
+    front_values(r)
+    loads[6].wait()
+    front_forward(r, r.act_out)
+    send_front = across(r, place, 0, r.act_out, r.arrive)
+    send_front.start()
+    for one in loads[9:13]:
+        one.wait()
+    r.unit_bias[0:1, 0:128] = r.bias_in[:, at(mine, 128)]
+    r.unit_bias[0:1, 128:256] = r.bias_in[:, at(half + mine, 128)]
+    hidden_tables(r)
+    for distance in range(1, 5):
+        cots.pass_on(distance)
+    for plane in range(4):
+        cots.settle(plane)
+    mine = hiddens.mine
+    near = mine + 1 - 2 * place.low
+    hiddens.wait(mine, hiddens.pair)
+    hiddens.open()
+    hiddens.pass_on(1)
+    hiddens.settle(mine)
+    hidden_plane(r, mine)
+    hiddens.pass_on(2)
+    across(r, place, 1, r.leave, r.arrive).wait_recv()
+
+    def matrix_done(j, value):
+        r.attn_out[j * 128 : (j + 1) * 128, :] = value
+
+    def patch_done(j, value):
+        r.patch_out[...] = value[0:24]
+        r.gift_patch[...] = value[24:48]
+
+    starts = (0, 256, 384, 0)
+
+    def matrix_of(which, target):
+        def room(j, level, start, rows):
+            if level == 3:
+                return r.last_room.at[at(j * 128 + start, rows)]
+            return r.rooms.at[which * 2 + j, at(starts[level] + start, rows)]
+
+        return Halving(
+            place,
+            lambda j, start, rows: r.grads.at[which * 2 + j, at(start, rows)],
+            room,
+            (256, 128, 128, 128),
+            r.sum_sent.at[:, at(which * 4, 4)],
+            r.sum_come.at[:, at(which * 4, 4)],
+            matrix_done,
+            target,
+        )
+
+    values, outs = matrix_of(0, (0, 1)), matrix_of(1, (1, 1))
+    patch_starts = (0, 384, 576, 672)
+    pixels = Halving(
+        place,
+        lambda j, start, rows: r.patch_sum.at[at(start, rows)],
+        lambda j, level, start, rows: r.patch_rooms.at[at(patch_starts[level] + start, rows)],
+        (384, 192, 96, 48),
+        r.patch_sent,
+        r.patch_come,
+        patch_done,
+    )
+    front_back_out(r, r.arrive)
+    outs.begin(0, 0)
+    outs.begin(1, 0)
+    front_back_values(r, r.arrive)
+    outs.finish(0, 0)
+    outs.finish(1, 0)
+    front_back_heads(r)
+    outs.finish(0, 1)
+    outs.finish(1, 1)
+    front_back_inputs(r, r.input_out, r.gift_half)
+    give_half = across(r, place, 2, r.gift_half, r.gift_half)
+    give_half.start()
+    hiddens.pass_on(3)
+    front_back_table(r)
+    front_back_projection(r)
+    values.begin(0, 0)
+    values.begin(1, 0)
+    outs.finish(0, 2)
+    outs.finish(1, 2)
+    front_back_pixels(r)
+    values.finish(0, 0)
+    values.finish(1, 0)
+    r.small[66:72, :] = jnp.zeros((6, D), F32)
+    smalls = Doubling(r, place, 72, r.small_sent, r.small_come)
+    smalls.begin()
+    front_back_order(r)
+    pixels.begin(0, 0)
+    outs.finish(0, 3)
+    outs.finish(1, 3)
+    hiddens.pass_on(4)
+    smalls.finish(0)
+    pixels.finish(0, 0)
+    hiddens.settle(near)
+    hidden_plane(r, near)
+    values.finish(0, 1)
+    values.finish(1, 1)
+    smalls.finish(1)
+    pixels.finish(0, 1)
+    far = mine + 2 - 4 * place.high
+    hiddens.settle(far)
+    hidden_plane(r, far)
+    values.finish(0, 2)
+    values.finish(1, 2)
+    smalls.finish(2)
+    pixels.finish(0, 2)
+    both = 3 - mine
+    hiddens.settle(both)
+    hidden_plane(r, both)
+    r.gift[0] = r.unit_two[128:256, :].astype(BF)
+    r.gift[1] = r.d_mid[128:256, :].astype(BF)
+    bias = col_sum(r.bias_sum[...].T)
+    r.gift_bias[...] = jnp.broadcast_to(bias[:, 128:256], (8, 128))
+    gifts = [across(r, place, 3, r.gift, r.gift), across(r, place, 4, r.gift_bias, r.gift_bias)]
+    for one in gifts:
+        one.start()
+    smalls.finish(3)
+    give_var = across(r, place, 5, r.small_in.at[3, 0:48], r.gift_var)
+    give_var.start()
+    pixels.finish(0, 3)
+    give_patch = across(r, place, 6, r.gift_patch, r.gift_patch)
+    give_patch.start()
+    r.win_out[...] = r.unit_two[0:128, :].T
+    r.wout_out[...] = r.d_mid[0:128, :]
+    r.bias_out[...] = bias[:, 0:128]
+    r.var_out[...] = r.small_in[3, 0:48]
+    front_tail(r, place)
+    values.finish(0, 3)
+    values.finish(1, 3)
+    take_small = across(r, place, 7, r.small_in.at[3, 0:16], r.gift_var.at[0:16])
+    take_small.wait_recv()
+    r.gain_out[...] = r.gift_var[4:6, :]
+    r.shift_out[...] = r.gift_var[6:9, :]
+    give_attn = pltpu.make_async_copy(r.attn_out, r.attn_final, r.loads.at[13])
+    give_attn.start()
+    cots.close()
+    hiddens.close()
+    for j in range(2):
+        values.close(j)
+        outs.close(j)
+    pixels.close(0)
+    smalls.close()
+    for one in (send_front, give_half, *gifts, give_var, give_patch):
+        one.wait_send()
+    give_attn.wait()
+
+
+def trunk_section(r, place):
+    def load(number, source, target):
+        return pltpu.make_async_copy(source, target, r.loads.at[number])
+
+    outs = [load(n, r.mlp_out.at[n * 1024 : (n + 1) * 1024], r.bufs.at[1, n]) for n in range(4)]
+    cots = [load(4 + n, r.cot_in.at[n], r.cot.at[n * 128 : (n + 1) * 128]) for n in range(2)]
+    attns = [load(6 + n, r.attn_in.at[0, n], r.attn.at[n]) for n in range(4)]
+    ins = [load(10 + n, r.mlp_in.at[:, n * 1024 : (n + 1) * 1024], r.bufs.at[0, n]) for n in range(4)]
+    for one in (*cots, *outs, *attns, *ins):
+        one.start()
+    r.small[0:24, :] = jnp.zeros((24, D), F32)
+    greet(place)
+    for one in (*cots, *outs):
+        one.wait()
+    trunk_ahead(r)
+    for one in (*attns, *ins):
+        one.wait()
+    across(r, place, 0, r.act_out, r.arrive).wait_recv()
+    trunk_attention(r, r.arrive)
+    plane, pair = place.plane(0), place.y * 2 + place.c
+    send_x = remote(
+        r.second,
+        r.bufs.at[0, plane, at(pair * 256, 256)],
+        r.over_sent.at[0],
+        r.x_come.at[plane * 4 + pair],
+        place.across,
+    )
+    send_x.start()
+    trunk_hidden(r)
+    send_x.wait_send()
+    trunk_back(r, r.leave)
+    send_in = across(r, place, 1, r.leave, r.arrive)
+    send_in.start()
+    trunk_out(r, r.act_out)
+    for level, device in enumerate(place.levels()):
+        pl.semaphore_signal(r.ready.at[level], inc=1, device_id=device, device_id_type=MESH)
+    smalls = Doubling(r, place, 16, r.small_sent, r.small_come)
+    smalls.begin()
+    trunk_weights(r)
+    for level in range(4):
+        pl.semaphore_wait(r.ready.at[level], 1)
+
+    def matrix_done(j, value):
+        r.attn_out[j * 64 : (j + 1) * 64, :] = value
+
+    starts = (0, 512, 768, 896)
+    matrices = Halving(
+        place,
+        lambda j, start, rows: r.bufs.at[0, j, at(start, rows)],
+        lambda j, level, start, rows: r.bufs.at[1, j, at(starts[level] + start, rows)],
+        (512, 256, 128, 64),
+        r.sum_sent.at[:, 0:4],
+        r.sum_come.at[:, 0:4],
+        matrix_done,
+    )
+    for j in range(4):
+        matrices.begin(j, 0)
+    for level in range(4):
+        smalls.finish(level)
+    send_small = across(r, place, 7, r.small_in.at[3, 0:16], r.gift_var.at[0:16])
+    send_small.start()
+    for turn in range(7):
+        for level in range(4):
+            if 0 <= turn - level < 4:
+                matrices.finish(turn - level, level)
+    give_attn = pltpu.make_async_copy(r.attn_out, r.attn_final, r.loads.at[14])
+    give_attn.start()
+    own = at((place.y * 2 + place.c) * 256, 256)
+    r.vec_out[...] = r.small_in[3, pl.ds(place.high * 2 + place.low, 1), own]
+    r.gain_out[...] = r.small_in[3, 4:6]
+    r.shift_out[...] = r.small_in[3, 6:9]
+    across(r, place, 2, r.gift_half, r.gift_half).wait_recv()
+    r.input_out[...] = r.gift_half[...].astype(F32)
+    across(r, place, 3, r.gift, r.gift).wait_recv()
+    across(r, place, 4, r.gift_bias, r.gift_bias).wait_recv()
+    r.win_out[...] = r.gift[0].astype(F32).T
+    r.wout_out[...] = r.gift[1].astype(F32)
+    r.bias_out[...] = r.gift_bias[0:1, :]
+    across(r, place, 5, r.small_in.at[3, 0:48], r.gift_var).wait_recv()
+    r.var_out[...] = r.gift_var[...]
+    across(r, place, 6, r.gift_patch, r.gift_patch).wait_recv()
+    r.patch_out[...] = r.gift_patch[...]
+    for j in range(4):
+        matrices.close(j)
+    smalls.close()
+    send_in.wait_send()
+    send_small.wait_send()
+    give_attn.wait()
+
+
+CELL_ROWS = (CELLS, D)
+SCRATCH = dict(
+    attn=((4, D, D), BF),
+    bufs=((2, 4, D, D), BF),
+    grads=((4, 512, D), BF),
+    rooms=((4, 512, D), BF),
+    last_room=((256, D), BF),
+    patch_rooms=((720, D), BF),
+    table=((WIDE, D), BF),
+    mid=((WIDE, D), BF),
+    turned=((D, WIDE), BF),
+    pat=((CELLS, WIDE), BF),
+    qhead=((32, D), BF),
+    fold=((16, D), BF),
+    fold_sum=((32, D), BF),
+    query_pair=((16, D), BF),
+    query_row=((8, D), F32),
+    score=((16, WIDE), F32),
+    uses=((16, 1, WIDE), F32),
+    probs=((32, 128, 128), F32),
+    resid=(CELL_ROWS, F32),
+    unit_one=(CELL_ROWS, F32),
+    unit_two=(CELL_ROWS, F32),
+    d_mid=(CELL_ROWS, F32),
+    rstd_one=((CELLS, LANES), F32),
+    rstd_two=((CELLS, LANES), F32),
+    normed=(CELL_ROWS, BF),
+    k=(CELL_ROWS, BF),
+    v=(CELL_ROWS, BF),
+    mixed=(CELL_ROWS, BF),
+    d_low=(CELL_ROWS, BF),
+    arrive=(CELL_ROWS, BF),
+    turn_a=((D, CELLS), BF),
+    turn_b=((D, CELLS), BF),
+    small=((72, D), F32),
+    small_in=((4, 72, D), F32),
+    unit_bias=((16, 256), BF),
+    gift=((2, 128, D), BF),
+    gift_bias=((8, 128), F32),
+    gift_patch=((24, D), F32),
+    gift_half=((CELLS, 384), BF),
+    gift_var=((48, D), F32),
+)
+SEMAPHORES = dict(
+    loads=(15,),
+    over_sent=(8,),
+    over_come=(8,),
+    cot_sent=(18,),
+    cot_come=(16,),
+    x_sent=(18,),
+    x_come=(16,),
+    sum_sent=(4, 8),
+    sum_come=(4, 8),
+    patch_sent=(1, 4),
+    patch_come=(1, 4),
+    small_sent=(4,),
+    small_come=(4,),
+)
+INPUTS = dict(
+    patches_in=pl.ANY,
+    masks=pltpu.VMEM,
+    leads=pltpu.SMEM,
+    cot_in=pl.ANY,
+    weight_in=pl.ANY,
+    embed=pltpu.VMEM,
+    attn_in=pl.ANY,
+    vecs=pltpu.VMEM,
+    gains=pltpu.VMEM,
+    shifts=pltpu.VMEM,
+    mlp_in=pl.ANY,
+    bias=pltpu.VMEM,
+    bias_in=pltpu.VMEM,
+    mlp_out=pl.ANY,
+)
+OUTPUTS = dict(
+    act_out=(CELL_ROWS, BF),
+    input_out=((CELLS, 384), F32),
+    patch_out=((24, D), F32),
+    var_out=((48, D), F32),
+    attn_final=(CELL_ROWS, F32),
+    vec_out=((1, 256), F32),
+    gain_out=((2, D), F32),
+    shift_out=((3, D), F32),
+    win_out=((D, 128), F32),
+    bias_out=((1, 128), F32),
+    wout_out=((128, D), F32),
+)
+
+
+class Refs:
+    pass
+
+
+def fused_kernel(*refs):
+    r = Refs()
+    names = list(INPUTS) + list(OUTPUTS) + list(SCRATCH) + list(SEMAPHORES) + ["ready"]
+    for name, ref in zip(names, refs, strict=True):
+        setattr(r, name, ref)
+    r.patch_sum = r.table.at[0:768]
+    r.raw = r.turned.at[0:768, 0:D]
+    for number, name in enumerate(("cot", "q", "second", "leave")):
+        setattr(r, name, r.turned.at[number * 256 : number * 256 + 256, 0:D])
+    r.pix = r.normed.at[:, 0 : V * PIX]
+    r.input_sum = r.resid
+    r.attn_out = r.resid
+    r.agg = r.mixed
+    r.dlow = r.d_low
+    r.wout = r.k
+    r.win_t = r.v
+    r.win = r.turn_a
+    r.keep = r.rstd_one
+    r.units = r.unit_one.at[:, 0:256]
+    r.bias_sum = r.unit_one.at[:, 256:512]
+    place = Place()
+    pl.when(place.section == 0)(lambda: front_section(r, place))
+    pl.when(place.section == 1)(lambda: trunk_section(r, place))
+
+
+def fused_shards(
+    patches,
+    masks,
+    lead_times,
+    cotangent,
+    patch_weight,
+    var_embed,
+    attention,
+    attn_vectors,
+    norm_gains,
+    trunk_shifts,
+    mlp_in,
+    mlp_in_bias,
+    mlp_out,
+):
+    outs = pl.pallas_call(
+        fused_kernel,
+        in_specs=[pl.BlockSpec(memory_space=space) for space in INPUTS.values()],
+        out_specs=[
+            pl.BlockSpec(memory_space=pl.ANY if one == (CELL_ROWS, F32) else pltpu.VMEM)
+            for one in OUTPUTS.values()
+        ],
+        out_shape=[jax.ShapeDtypeStruct(*one) for one in OUTPUTS.values()],
+        scratch_shapes=[pltpu.VMEM(*one) for one in SCRATCH.values()]
+        + [pltpu.SemaphoreType.DMA(one) for one in SEMAPHORES.values()]
+        + [pltpu.SemaphoreType.REGULAR((4,))],
+        compiler_params=pltpu.CompilerParams(
+            collective_id=0, has_side_effects=True, vmem_limit_bytes=60 * 2**20
+        ),
+    )(
+        patches,
+        masks,
+        lead_times,
+        cotangent,
+        patch_weight,
+        var_embed,
+        attention,
+        attn_vectors[0],
+        norm_gains,
+        trunk_shifts,
+        mlp_in,
+        mlp_in_bias.reshape(4, 1, D),
+        mlp_in_bias.reshape(1, FF),
+        mlp_out,
+    )
+    act, inputs, patch, var, attn, vec, gain, shift, win, bias, wout = outs
+    return (
+        act.reshape(1, 2, 128, D),
+        inputs.reshape(2, 128, 384),
+        patch,
+        var,
+        attn[None],
+        vec,
+        gain,
+        shift,
+        win,
+        bias.reshape(128),
+        wout,
+    )
+
+
 def solution(mesh):
     in_specs = (
         P("dp", None, None),
@@ -512,4 +1693,6 @@
         P(("section", "dp")),
         P(("section", "dp"), None),
     )
-    return jax.shard_map(shards, mesh=mesh, in_specs=in_specs, out_specs=out_specs, check_vma=False)
+    small = mesh.shape["section"] == 2 and mesh.shape["dp"] == 16
+    body = fused_shards if small else shards
+    return jax.shard_map(body, mesh=mesh, in_specs=in_specs, out_specs=out_specs, check_vma=False)

time: 1500 us -> 219 us (0.15)
  waiting for transfers between devices: 762 us -> 0 us
  blocking collectives: 441 us -> 0 us
  Pallas kernels: 0 us -> 198 us
  matrix products: 147 us -> 0 us
  local copies, waits for them, and re-layouts: 60.6 us -> 20.4 us
  loops' own time: 28.7 us -> 0 us
  other arithmetic: 27.6 us -> 0 us
  between operations: 15.8 us -> 0.66 us
    reduce_scatter x4 -> x0, waiting for transfers between devices: 591 us -> none  [the longest x1 188 us: shards(): lax.psum_scatter(carried['w_in'], ('section', 'dp'), scatter_dimension=1,...]
    psum x1 -> x0, blocking collectives: 441 us -> none  [shards(): lax.psum((carried['var'], carried['gains'], carried['shifts']), ('section...]
    pallas_call x0 -> x1, Pallas kernels: none -> 198 us  [fused_shards(): pl.pallas_call(fused_kernel, in_specs=[pl.BlockSpec(memory_space=space) f...]
    dot_general x46 -> x0, matrix products: 144 us -> none  [the longest x12 57.5 us: matmul_tn(): lax.dot_general(left_side, right_side, (((0,), (0,)), ((), ())), preferre...]
    ppermute x4 -> x0, waiting for transfers between devices: 82 us -> none  [from_behind(): lax.ppermute(value, axis, [(source, source + steps) for source in range(l...]
    psum x1 -> x0, waiting for transfers between devices: 73.4 us -> none  [shards(): lax.psum((carried['var'], carried['gains'], carried['shifts']), ('section...]
    another operation x5 -> x0, loops' own time: 28.7 us -> none  [the longest x3 23.3 us: shards(): lax.cond(on_front, front_turn, back_turn, (carried, arriving_act))]
    another operation x8 -> x0, local copies, waits for them, and re-layouts: 24 us -> none
  transfers between devices with their start and end apart: 10 -> 0, of which waited for: 9 -> 0; matrix products, arithmetic and copies ran while one was open for 0% -> 0% of each run, Pallas kernels for 0% -> 0%
where the time goes in v1:
time: 219 us
  Pallas kernels  198 us (90%)
  local copies, waits for them, and re-layouts  20.4 us (9%)
    pallas_call x1, Pallas kernels, fused_shards(): pl.pallas_call(fused_kernel, in_specs=[pl.BlockSpec(memory_space=space) f...  198 us
    unnamed x11, local copies, waits for them, and re-layouts  17.8 us

profile of v1, /device:TPU:19, one launch (start us, length us, event | category | flops | bytes accessed | tf_op | source)
XLA Modules:
  0.0 218.7 jit_solution(1802468832818423494)
XLA Ops:
  0.6 1.3 reshape.38.refs_12_
  2.0 1.3 reshape.42.refs_11_
  3.3 197.6 %shard_map.212 = (bf16[256,1024]{1,0:T(8,128)(2,1)}, f32[256,384]{1,0:T(8,128)}, f32[24,1024]{1,0:T(8,128)}, f32[48,1024]{1,0:T(8,128)}, f32[256,1024]{1,0:T(8,1...) custom-call(bf16[2,128,768]{2,1,0:T(8,128)(2,1)} %refs_0_.1, ...), custom_call_target="tpu_custom_call" | custom-call | tf_op jit(solution)/shard_map/pallas_call | solution.py:1621
  200.9 1.9 copy.36
  202.8 1.8 copy.37
  204.6 1.5 copy.38
  206.1 1.6 copy.39
  207.7 2.3 %copy.40 = f32[1,256,1024]{2,1,0:T(8,128)} copy(f32[1,256,1024]{2,1,0:T(8,128)} %bitcast.5) | data formatting | bytes 2097152
  210.0 1.2 copy.41
  211.2 1.3 copy.42
  212.5 1.3 copy.43
  213.8 1.9 copy.44
  215.7 1.1 copy.45
  216.8 1.9 copy.46
